TPU v7x, 32 devices: a whole 2x2x4 slice. The times are simulated.
32 devices in a mesh: groups: 2 (over x), dp: 2 (over core), tensor: 8 (over z, y).
Axes of the slice: x: 2, y: 2, z: 4, core: 2. Of those that a mesh axis runs over, the one named last changes fastest.
Arguments:
- expert_hidden: bfloat16 [512, 8192], P(('groups', 'dp'), 'tensor'), parts along dimension 0, may hold values from -6 to 6
- expert_gain: float32 [8192], replicated, may hold values from 0.5 to 1.5
- expert_output_weight: bfloat16 [8192, 16384], P('dp', 'tensor'), may hold values from -0.0625 to 0.0625
- small_hidden: bfloat16 [2, 512, 4096], P(None, ('groups', 'dp'), 'tensor'), parts along dimension 1, may hold values from -100 to 100
- minor_norm_gains: float32 [2, 4096], P(None, 'tensor'), may hold values from 0.5 to 1.5
- minor_output_weights: bfloat16 [2, 4096, 16384], P(None, 'tensor', 'dp'), may hold values from -0.125 to 0.125
Outputs:
- steered_logits: float32 [512, 16384], P(('groups', 'dp'), 'tensor'), parts along dimension 0
There are 2 independent parts, one for each index of `groups`. A program takes and returns all parts, laid end to end along the dimension named above; an argument that names none is the same for every part. Nothing has to cross between parts.
All inputs are finite; a program needn't handle non-finite values.
Results may differ from a plain program's by a relative error of at most 0.0029.
Values may be sent and summed in bfloat16 or wider, within the bound.
A program may use at most 256 MiB of HBM per device.

v0:
```python
import jax
import jax.numpy as jnp
from jax import lax
from jax.sharding import PartitionSpec as P

DS = 4096


def on_device(
    expert_hidden,
    expert_gain,
    expert_output_weight,
    small_hidden,
    minor_norm_gains,
    minor_output_weights,
):
    features_all = lax.all_gather(expert_hidden, "tensor", axis=1, tiled=True)
    values = features_all.astype(jnp.float32)
    mean_sq = jnp.mean(values * values, axis=-1, keepdims=True)
    expert_normed = (values * lax.rsqrt(mean_sq + 1e-05) * expert_gain).astype(jnp.bfloat16)
    expert_logits = jnp.dot(
        expert_normed,
        lax.all_gather(expert_output_weight, "dp", axis=0, tiled=True),
        preferred_element_type=jnp.float32,
    )
    local = small_hidden.astype(jnp.float32)
    totals = lax.psum(jnp.sum(local * local, axis=-1), "tensor")
    scales = lax.rsqrt(totals / DS + 1e-05)
    minor_normed_hidden = (local * scales[:, :, None] * minor_norm_gains[:, None, :]).astype(
        jnp.bfloat16
    )
    partial_product = jnp.einsum(
        "dpg,dgz->dpz",
        minor_normed_hidden,
        lax.all_gather(minor_output_weights, "dp", axis=2, tiled=True),
        preferred_element_type=jnp.float32,
    )
    pieces = (partial_product[0], partial_product[1])
    adjusted_logits, baseline = (
        lax.psum_scatter(pieces[0], "tensor", scatter_dimension=1, tiled=True),
        lax.psum_scatter(pieces[1], "tensor", scatter_dimension=1, tiled=True),
    )
    offset = adjusted_logits - baseline
    return expert_logits + offset


def solution(mesh):
    in_specs = (
        P(("groups", "dp"), "tensor"),
        P(),
        P("dp", "tensor"),
        P(None, ("groups", "dp"), "tensor"),
        P(None, "tensor"),
        P(None, "tensor", "dp"),
    )
    out_specs = P(("groups", "dp"), "tensor")
    return jax.shard_map(
        on_device, mesh=mesh, in_specs=in_specs, out_specs=out_specs, check_vma=False
    )
```

profile of v0, /device:TPU:4, one launch (start us, length us, event | category | flops | bytes accessed | tf_op | source)
XLA Modules:
  0.0 495.5 jit_solution(6358678813690258654)
XLA Ops:
  6.5 0.0 all-gather.8.cloned.1.call-start
  6.5 0.7 all-gather.8.cloned.1.call-update
  7.3 0.0 all-gather.4.cloned.1.call-start
  7.3 0.7 all-gather.4.cloned.1.call-update
  8.0 0.0 copy-start
  8.0 0.0 copy-start.2
  8.0 0.0 all-gather.6.cloned.1.call-start
  8.1 0.7 all-gather.6.cloned.1.call-update
  8.8 0.0 reduce-scatter.3.cloned.1.call-start
  8.8 0.1 copy-done
  9.0 0.1 fusion.6
  9.1 18.0 %psum.7 = f32[2,128]{1,0:T(2,128)S(1)} all-reduce(f32[2,128]{1,0:T(2,128)S(1)} %fusion.6), channel_id=1, replica_groups=mesh['groups'=2,'dp'=2,'tensor'=8] {'tensor'}, use_global_device_ids=true, to_apply=%region_2.0 | all-reduce | flops 256 | bytes 2048 | tf_op jit(solution)/shard_map/psum | solution.py:27
  27.1 34.6 %all-gather.8.cloned.1.call-done = bf16[2,512,16384]{2,1,0:T(8,128)(2,1)} async-done(((bf16[2,512,8192]{2,1,0:T(8,128)(2,1)}), bf16[2,512,16384]{2,1,0:T(8,128)(2,1)}) %all-gather.8.cloned.1.call-update) | async-done | bytes 33554448 | tf_op jit(solution)/shard_map/all_gather | solution.py:35
  61.6 0.0 copy-done.2
  61.6 20.9 %fusion.9 = f32[2,128,16384]{2,1,0:T(8,128)} fusion(bf16[2,512,16384]{2,1,0:T(8,128)(2,1)} %all-gather.8.cloned.1.call-done, bf16[2,128,512]{2,1,0:T(8,128)(2,1)S(1)} %copy-done, f32[2,512]{1,0:T(2,128)S(1)} %copy-done.2, f32[2,128]{1,0:T(2,128)S(1)} %add_rsqrt_fusion), kind=kOutput, calls=%fused_computation.15 | convolution fusion | flops 4295491584 | bytes 50598912 | tf_op jit(solution)/shard_map/dpg,dgz->dpz/dot_general | solution.py:32
  82.6 11.4 %slice_bitcast_fusion = (f32[128,16384]{1,0:T(8,128)}, f32[128,16384]{1,0:T(8,128)}) fusion(f32[2,128,16384]{2,1,0:T(8,128)} %fusion.9), kind=kLoop, calls=%fused_computation | loop fusion | bytes 33554432 | tf_op jit(solution)/shard_map/squeeze | solution.py:38
  94.0 0.0 copy-start.1
  94.0 0.0 reduce-scatter.3.cloned.1.call-update
  94.0 0.0 reduce-scatter.5.cloned.1.call-start
  94.0 0.5 reduce-scatter.5.cloned.1.call-update
  94.6 18.5 %all-gather.4.cloned.1.call-done = bf16[128,8192]{1,0:T(8,128)(2,1)} async-done(((bf16[128,1024]{1,0:T(8,128)(2,1)}), bf16[128,8192]{1,0:T(8,128)(2,1)}) %all-gather.4.cloned.1.call-update) | async-done | bytes 2097168 | tf_op jit(solution)/shard_map/all_gather | solution.py:17
  113.1 2.1 fusion
  115.2 50.4 %all-gather.6.cloned.1.call-done = bf16[8192,2048]{1,0:T(8,128)(2,1)} async-done(((bf16[4096,2048]{1,0:T(8,128)(2,1)}), bf16[8192,2048]{1,0:T(8,128)(2,1)}) %all-gather.6.cloned.1.call-update) | async-done | bytes 33554448 | tf_op jit(solution)/shard_map/all_gather | solution.py:23
  165.6 153.8 %reduce-scatter.3.cloned.1.call-done = f32[128,2048]{1,0:T(8,128)} async-done(((f32[128,16384]{1,0:T(8,128)}), f32[128,2048]{1,0:T(8,128)}) %reduce-scatter.3.cloned.1.call-update) | async-done | bytes 1048592 | tf_op jit(solution)/shard_map/reduce_scatter | solution.py:40
  319.4 152.4 %reduce-scatter.5.cloned.1.call-done = f32[128,2048]{1,0:T(8,128)} async-done(((f32[128,16384]{1,0:T(8,128)}), f32[128,2048]{1,0:T(8,128)}) %reduce-scatter.5.cloned.1.call-update) | async-done | bytes 1048592 | tf_op jit(solution)/shard_map/reduce_scatter | solution.py:41
  471.8 0.0 copy-done.1
  471.8 17.2 %convolution_add_fusion = f32[128,2048]{1,0:T(8,128)} fusion(bf16[8192,2048]{1,0:T(8,128)(2,1)} %all-gather.6.cloned.1.call-done, bf16[128,8192]{1,0:T(8,128)(2,1)} %all-gather.4.cloned.1.call-done, f32[8192]{0:T(1024)S(1)} %copy-done.1, f32[128]{0:T(128)S(1)} %add_rsqrt_fusion.1, f32[128,2048]{1,0:T(8,128)} %reduce-scatter.3.cloned.1.call-done, ...), kind=kOutput, calls=%fused_computation.7 | convolution fusion | flops 4299685888 | bytes 38830592 | tf_op jit(solution)/shard_map/dot_general | solution.py:21
  (2 shorter events, 0.0 us)
Async XLA Ops:
  6.5 55.1 %all-gather.8.cloned.1.call-start = ((), (), s32[]{:S(2)}) async-start(), calls=%async_computation.4 | async-start | bytes 50331648 | tf_op jit(solution)/shard_map/all_gather | solution.py:35
  7.3 105.9 %all-gather.4.cloned.1.call-start = ((), (), s32[]{:S(2)}) async-start(), calls=%async_computation.2 | async-start | bytes 2359296 | tf_op jit(solution)/shard_map/all_gather | solution.py:17
  8.0 1.0 copy-start
  8.0 53.6 %copy-start.2 = (f32[2,512]{1,0:T(2,128)S(1)}, f32[2,512]{1,0:T(2,128)}, u32[]{:S(2)}) copy-start(f32[2,512]{1,0:T(2,128)} %param.10) | copy-start | bytes 12292
  8.0 157.6 %all-gather.6.cloned.1.call-start = ((), (), s32[]{:S(2)}) async-start(), calls=%async_computation.3 | async-start | bytes 50331648 | tf_op jit(solution)/shard_map/all_gather | solution.py:23
  8.8 310.7 %reduce-scatter.3.cloned.1.call-start = ((), (), s32[]{:S(2)}) async-start(), calls=%async_computation.5 | async-start | bytes 9437184 | tf_op jit(solution)/shard_map/reduce_scatter | solution.py:40
  94.0 377.8 %copy-start.1 = (f32[8192]{0:T(1024)S(1)}, f32[8192]{0:T(1024)}, u32[]{:S(2)}) copy-start(f32[8192]{0:T(1024)} %param.7) | copy-start | bytes 98308
  94.0 377.8 %reduce-scatter.5.cloned.1.call-start = ((), (), s32[]{:S(2)}) async-start(), calls=%async_computation.6 | async-start | bytes 9437184 | tf_op jit(solution)/shard_map/reduce_scatter | solution.py:41
Sparse Core Ops, SparseCore 0:
  8.9 52.6 all-gather.7
  63.8 49.2 all-gather.3
  114.7 50.8 all-gather.5
  169.1 150.2 reduce-scatter.2
  323.3 148.4 reduce-scatter.4
where the time goes:
time: 497 us; the launch traced here: 496 us
  waiting for transfers between devices  412 us (83%)
  matrix products  38.1 us (8%)
  blocking collectives  18 us (4%)
  between operations  13.2 us (3%)
  local copies, waits for them, and re-layouts  11.5 us (2%)
    reduce_scatter x1, waiting for transfers between devices, on_device(): lax.psum_scatter(pieces[0], 'tensor', scatter_dimension=1, tiled=True)  154 us
    reduce_scatter x1, waiting for transfers between devices, on_device(): lax.psum_scatter(pieces[1], 'tensor', scatter_dimension=1, tiled=True)  152 us
    all_gather x1, waiting for transfers between devices, on_device(): lax.all_gather(expert_output_weight, 'dp', axis=0, tiled=True)  50.4 us
    all_gather x1, waiting for transfers between devices, on_device(): lax.all_gather(minor_output_weights, 'dp', axis=2, tiled=True)  34.6 us
    dot_general x1, matrix products, on_device(): jnp.einsum('dpg,dgz->dpz', minor_normed_hidden, lax.all_gather(minor_outp...  20.9 us
    all_gather x1, waiting for transfers between devices, on_device(): features_all = lax.all_gather(expert_hidden, 'tensor', axis=1, tiled=True)  18.5 us
    psum x1, blocking collectives, on_device(): totals = lax.psum(jnp.sum(local * local, axis=-1), 'tensor')  18 us
    dot_general x1, matrix products, on_device(): jnp.dot(expert_normed, lax.all_gather(expert_output_weight, 'dp', axis=0,...  17.2 us
  transfers between devices with their start and end apart: 5, of which 5 were waited for; matrix products, arithmetic and copies ran while one was open for 7% of the time, Pallas kernels for 0%

commit v1 on v0

v1 whole, which is shorter than its diff:
```python
import functools

import jax
import jax.numpy as jnp
from jax import lax
from jax.experimental import pallas as pl
from jax.experimental.pallas import tpu as pltpu
from jax.sharding import PartitionSpec as P

F32 = jnp.float32
BF16 = jnp.bfloat16
EPS = 1e-05


def kernel(
    T, D, DS, ns,
    xe_ref, gain_ref, xs_ref, sgain_ref, we_hbm, ws_hbm, out_ref,
    we_v, ws_v, xe_n, act_e, act_s, stat_out, stat_in, ysend, yrecv, own, zsend, zrecv, epart, erecv,
    we_sem, ws_sem, st_s, st_r, as_s, as_r, eA_s, eA_r, eC_s, eC_r, y_s, y_r, z_s, z_r, ep_s, ep_r,
):
    Z = T // 2
    h = Z // 2
    R, De = xe_n.shape
    Ds = xs_ref.shape[2]
    Vt = out_ref.shape[1]
    sub = Vt // ns
    col = min(512, sub)
    c = lax.axis_index("dp")
    t = lax.axis_index("tensor")
    z = t // 2
    y = t % 2
    oc = 1 - c
    oy = 1 - y
    lo = c * h
    below = z < lo + h // 2
    cz = z // h
    zk = z % h

    def dev(cc, yy, zz):
        return {"dp": cc, "tensor": zz * 2 + yy}

    def rcopy(src, dst, s, r, d):
        return pltpu.make_async_remote_copy(
            src_ref=src, dst_ref=dst, send_sem=s, recv_sem=r, device_id=d,
            device_id_type=pl.DeviceIdType.MESH,
        )

    def arrived(ref, sem):
        pltpu.make_async_copy(ref, ref, sem).wait()

    far = [jnp.where(below, h - 1 - i, i) for i in range(h)]
    near = [jnp.where(below, i, h - 1 - i) for i in range(h)]

    def ws_copy(chunk):
        return pltpu.make_async_copy(
            ws_hbm.at[:, pl.ds(pl.multiple_of(chunk * Vt, Vt), Vt)], ws_v.at[chunk], ws_sem.at[chunk]
        )

    we_copy = pltpu.make_async_copy(we_hbm, we_v, we_sem)
    for yy in (oy, y):
        for k in far:
            ws_copy(k * 2 + yy).start()
    we_copy.start()

    barrier = pltpu.get_barrier_semaphore()

    @pl.loop(1, 2 * T)
    def _(i):
        other = lax.rem(c * T + t + i, 2 * T)
        pl.semaphore_signal(
            barrier, inc=1, device_id={"dp": other // T, "tensor": lax.rem(other, T)},
            device_id_type=pl.DeviceIdType.MESH,
        )

    xe = xe_ref[...].astype(F32)
    x0 = xs_ref[0].astype(F32)
    x1 = xs_ref[1].astype(F32)
    lane = lax.broadcasted_iota(jnp.int32, (R, 128), 1)
    se = jnp.sum(xe * xe, axis=-1, keepdims=True)
    s0 = jnp.sum(x0 * x0, axis=-1, keepdims=True)
    s1 = jnp.sum(x1 * x1, axis=-1, keepdims=True)
    packed = jnp.where(lane == 0, se, jnp.where(lane == 1, s0, jnp.where(lane == 2, s1, 0.0)))
    stat_out[...] = packed.T[0:8, :]

    pl.semaphore_wait(barrier, 2 * T - 1)

    def stat_copy(i):
        o = lax.rem(t + i, T)
        return rcopy(
            stat_out, stat_in.at[t], st_s.at[i], st_r.at[t], {"dp": c, "tensor": o}
        )

    @pl.loop(1, T)
    def _(i):
        stat_copy(i).start()

    total = stat_out[...]
    for i in range(1, T):
        o = lax.rem(t + i, T)
        arrived(stat_in.at[o], st_r.at[o])
        total = total + stat_in[o]
    row = lax.broadcasted_iota(jnp.int32, (8, R), 0)
    scale = lax.rsqrt(jnp.where(row == 0, total * (1.0 / D), total * (1.0 / DS)) + EPS)
    scale = jnp.concatenate([scale, jnp.zeros((R - 8, R), F32)], axis=0).T

    act_s[c, :, 0:Ds] = (x0 * scale[:, 1:2] * sgain_ref[0]).astype(BF16)
    act_s[c, :, Ds:2 * Ds] = -((x1 * scale[:, 2:3] * sgain_ref[1]).astype(BF16))
    as_copy = rcopy(act_s.at[c], act_s.at[c], as_s, as_r, dev(oc, y, z))
    as_copy.start()

    xe_n[...] = (xe * scale[:, 0:1] * gain_ref[t]).astype(BF16)
    across = rcopy(xe_n, act_e.at[zk, y, c], eA_s.at[1], eA_r.at[y, c], dev(cz, oy, z))
    across.start()
    to_core = rcopy(xe_n, act_e.at[zk, y, c], eA_s.at[0], eA_r.at[y, c], dev(cz, y, z))

    @pl.when(cz == c)
    def _():
        pltpu.make_async_copy(xe_n, act_e.at[zk, y, c], eA_r.at[y, c]).start()

    @pl.when(cz != c)
    def _():
        to_core.start()

    def onward(k, yy, up):
        return rcopy(
            act_e.at[k, yy], act_e.at[k, yy], eC_s.at[k, yy, up], eC_r.at[k, yy],
            dev(c, y, z + 1 if up else z - 1),
        )

    @pl.when(cz == c)
    def _():
        for yy in range(2):
            for cc in range(2):
                arrived(act_e.at[zk, yy, cc], eA_r.at[yy, cc])
            for up in range(2):
                @pl.when((z < Z - 1) if up else (z > 0))
                def _():
                    onward(zk, yy, up).start()

    as_copy.wait_recv()

    def small_tile(chunk, off):
        lhs = act_s[...].reshape(2 * R, 2 * Ds)
        return jnp.dot(lhs, ws_v[chunk, :, pl.ds(off, col)], preferred_element_type=F32)

    def y_copy(i, s):
        k = far[i]
        return rcopy(ysend.at[k, s], yrecv.at[k, s], y_s.at[k, s], y_r.at[k, s], dev(c, oy, z))

    for i in range(h):
        chunk = far[i] * 2 + oy
        ws_copy(chunk).wait()
        for s in range(ns):
            for j in range(sub // col):
                ysend[far[i], s, :, j * col:(j + 1) * col] = small_tile(chunk, s * sub + j * col).astype(BF16)
            y_copy(i, s).start()

    for i in range(h):
        chunk = far[i] * 2 + y
        ws_copy(chunk).wait()
        for s in range(ns):
            for j in range(sub // col):
                own[far[i], s, :, j * col:(j + 1) * col] = small_tile(chunk, s * sub + j * col)

    for i in range(h):
        k = near[i]
        zs = lo + k

        @pl.when(zs != z)
        def _():
            for yy in range(2):
                arrived(act_e.at[k, yy], eC_r.at[k, yy])
                @pl.when((zs < z) & (z < Z - 1))
                def _():
                    onward(k, yy, 1).start()

                @pl.when((zs > z) & (z > 0))
                def _():
                    onward(k, yy, 0).start()

    def z_copy(i, s, cc):
        k = far[i]
        return rcopy(
            zsend.at[k, s, cc], zrecv.at[z, s], z_s.at[k, s, cc], z_r.at[z, s], dev(cc, y, lo + k)
        )

    def home(i, cc):
        return (lo + far[i] == z) & (c == cc)

    for i in range(h):
        k = far[i]
        for s in range(ns):
            y_copy(i, s).wait_recv()
            for cc in range(2):
                zsend[k, s, cc] = (
                    own[k, s, cc * R:(cc + 1) * R, :] + yrecv[k, s, cc * R:(cc + 1) * R, :].astype(F32)
                ).astype(BF16)

                @pl.when(home(i, cc))
                def _():
                    pltpu.make_async_copy(zsend.at[k, s, cc], zrecv.at[z, s], z_r.at[z, s]).start()

                @pl.when(jnp.logical_not(home(i, cc)))
                def _():
                    z_copy(i, s, cc).start()

    we_copy.wait()
    ecol = min(512, Vt)

    @pl.loop(0, Vt // ecol)
    def _(j):
        at = pl.ds(pl.multiple_of(j * ecol, ecol), ecol)
        acc = jnp.zeros((2 * R, ecol), F32)
        for k in range(h):
            for yy in range(2):
                b = k * 2 + yy
                acc = acc + jnp.dot(
                    act_e[k, yy].reshape(2 * R, De), we_v[b * De:(b + 1) * De, at],
                    preferred_element_type=F32,
                )
        epart[0, :, at] = acc[0:R]
        epart[1, :, at] = acc[R:2 * R]

    ep_copy = rcopy(epart.at[oc], erecv, ep_s, ep_r, dev(oc, y, z))
    ep_copy.start()

    for zz in range(Z):
        for s in range(ns):
            arrived(zrecv.at[zz, s], z_r.at[zz, s])
    ep_copy.wait_recv()
    for s in range(ns):
        at = slice(s * sub, (s + 1) * sub)
        acc = zrecv[0, s].astype(F32)
        for zz in range(1, Z):
            acc = acc + zrecv[zz, s].astype(F32)
        out_ref[:, at] = acc + (epart[c, :, at] + erecv[:, at])

    @pl.loop(1, T)
    def _(i):
        stat_copy(i).wait_send()

    as_copy.wait_send()
    across.wait_send()

    @pl.when(cz != c)
    def _():
        to_core.wait_send()

    for i in range(h):
        k = near[i]
        zs = lo + k
        for yy in range(2):
            @pl.when((zs <= z) & (z < Z - 1))
            def _():
                onward(k, yy, 1).wait_send()

            @pl.when((zs >= z) & (z > 0))
            def _():
                onward(k, yy, 0).wait_send()
    for i in range(h):
        for s in range(ns):
            y_copy(i, s).wait_send()
            for cc in range(2):
                @pl.when(jnp.logical_not(home(i, cc)))
                def _():
                    z_copy(i, s, cc).wait_send()
    ep_copy.wait_send()


def on_device(T, xe, gain, we, xs, sgain, ws):
    R, De = xe.shape
    Ds = xs.shape[2]
    Dh, Vt = we.shape
    D, DS = De * T, Ds * T
    h = T // 4
    ns = 2 if Vt >= 1024 else 1
    sub = Vt // ns
    vmem = pl.BlockSpec(memory_space=pltpu.VMEM)
    hbm = pl.BlockSpec(memory_space=pl.ANY)
    dma = pltpu.SemaphoreType.DMA
    flops = 2 * 2 * R * (Dh * Vt + 2 * Ds * Vt * (T // 2))
    return pl.pallas_call(
        functools.partial(kernel, T, D, DS, ns),
        out_shape=jax.ShapeDtypeStruct((R, Vt), F32),
        in_specs=[vmem, vmem, vmem, vmem, hbm, hbm],
        out_specs=vmem,
        scratch_shapes=[
            pltpu.VMEM((Dh, Vt), BF16),
            pltpu.VMEM((T // 2, 2 * Ds, Vt), BF16),
            pltpu.VMEM((R, De), BF16),
            pltpu.VMEM((h, 2, 2, R, De), BF16),
            pltpu.VMEM((2, R, 2 * Ds), BF16),
            pltpu.VMEM((8, R), F32),
            pltpu.VMEM((T, 8, R), F32),
            pltpu.VMEM((h, ns, 2 * R, sub), BF16),
            pltpu.VMEM((h, ns, 2 * R, sub), BF16),
            pltpu.VMEM((h, ns, 2 * R, sub), F32),
            pltpu.VMEM((h, ns, 2, R, sub), BF16),
            pltpu.VMEM((T // 2, ns, R, sub), BF16),
            pltpu.VMEM((2, R, Vt), F32),
            pltpu.VMEM((R, Vt), F32),
            dma, dma((T // 2,)),
            dma((T,)), dma((T,)),
            dma, dma,
            dma((2,)), dma((2, 2)),
            dma((h, 2, 2)), dma((h, 2)),
            dma((h, ns)), dma((h, ns)),
            dma((h, ns, 2)), dma((T // 2, ns)),
            dma, dma,
        ],
        compiler_params=pltpu.CompilerParams(
            collective_id=0, has_side_effects=True, vmem_limit_bytes=60 * 1024 * 1024
        ),
        cost_estimate=pl.CostEstimate(flops=flops, bytes_accessed=2 * 2 * Dh * Vt, transcendentals=0),
    )(
        xe, gain.reshape(T, 1, De), xs, sgain.reshape(2, 1, Ds), we, ws.reshape(2 * Ds, ws.shape[2])
    )


def solution(mesh):
    in_specs = (
        P(("groups", "dp"), "tensor"),
        P(),
        P("dp", "tensor"),
        P(None, ("groups", "dp"), "tensor"),
        P(None, "tensor"),
        P(None, "tensor", "dp"),
    )
    out_specs = P(("groups", "dp"), "tensor")
    return jax.shard_map(
        functools.partial(on_device, mesh.shape["tensor"]),
        mesh=mesh, in_specs=in_specs, out_specs=out_specs, check_vma=False,
    )
```

time: 497 us -> 104 us (0.21)
  the two profiles are of different devices: /device:TPU:4 before, /device:TPU:21 now
where the time goes in v1:
time: 104 us
  Pallas kernels  101 us (97%)
  local copies, waits for them, and re-layouts  3.58 us (3%)
    pallas_call x1, Pallas kernels, on_device(): pl.pallas_call(functools.partial(kernel, T, D, DS, ns), out_shape=jax.Sha...  101 us
    unnamed x1, local copies, waits for them, and re-layouts  2.3 us

profile of v1, /device:TPU:21, one launch (start us, length us, event | category | flops | bytes accessed | tf_op | source)
XLA Modules:
  0.0 104.1 jit_solution(14323972913571770697)
XLA Ops:
  0.0 1.3 %reshape.10.sgain_ref = f32[2,1,512]{2,1,0:T(1,128)} reshape(f32[2,512]{1,0:T(2,128)} %param.10) | data formatting | bytes 8192 | tf_op jit(solution)/shard_map/reshape | solution.py:316
  1.3 100.5 %shard_map.64 = f32[128,2048]{1,0:T(8,128)} custom-call(bf16[128,1024]{1,0:T(8,128)(2,1)} %xe_ref.1, f32[8,1,1024]{2,1,0:T(1,128)} %bitcast.3, bf16[2,128,512]{2,1,0:T(8,128)(2,1)} %xs_ref.1, f32[2,1,512]{2,1,0:T(1,128)} %reshape.10.sgain_ref, bf16[4096,2048]{1,0:T(8,128)(2,1)} %we_hbm.1, bf16[1024,8192]{1,0:T(8,128)(2,1)} %bitcast.2), custom_call_target="tpu_custom_call" | custom-call | flops 8589934592 | bytes 33554432 | tf_op jit(solution)/shard_map/pallas_call | solution.py:282
  101.8 2.3 %copy.8 = f32[128,2048]{1,0:T(8,128)} copy(f32[128,2048]{1,0:T(8,128)} %shard_map.64) | data formatting | bytes 2097152

commit v2 on v1

--- a/solution.py
+++ b/solution.py
@@ -15,8 +15,8 @@
 def kernel(
     T, D, DS, ns,
     xe_ref, gain_ref, xs_ref, sgain_ref, we_hbm, ws_hbm, out_ref,
-    we_v, ws_v, xe_n, act_e, act_s, stat_out, stat_in, ysend, yrecv, own, zsend, zrecv, epart, erecv,
-    we_sem, ws_sem, st_s, st_r, as_s, as_r, eA_s, eA_r, eC_s, eC_r, y_s, y_r, z_s, z_r, ep_s, ep_r,
+    we_v, ws_v, xe_n, act_e, act_s, stat_out, stat_in, ysend, yrecv, own, zsend, zrecv, psend, precv, epart, erecv,
+    we_sem, ws_sem, st_s, st_r, as_s, as_r, eA_s, eA_r, eC_s, eC_r, y_s, y_r, z_s, z_r, p_s, p_r, ep_s, ep_r,
 ):
     Z = T // 2
     h = Z // 2
@@ -103,8 +103,8 @@
     scale = lax.rsqrt(jnp.where(row == 0, total * (1.0 / D), total * (1.0 / DS)) + EPS)
     scale = jnp.concatenate([scale, jnp.zeros((R - 8, R), F32)], axis=0).T
 
-    act_s[c, :, 0:Ds] = (x0 * scale[:, 1:2] * sgain_ref[0]).astype(BF16)
-    act_s[c, :, Ds:2 * Ds] = -((x1 * scale[:, 2:3] * sgain_ref[1]).astype(BF16))
+    act_s[c, :, 0:Ds] = (x0 * scale[:, 1:2] * sgain_ref[0:1, :]).astype(BF16)
+    act_s[c, :, Ds:2 * Ds] = -((x1 * scale[:, 2:3] * sgain_ref[1:2, :]).astype(BF16))
     as_copy = rcopy(act_s.at[c], act_s.at[c], as_s, as_r, dev(oc, y, z))
     as_copy.start()
 
@@ -162,47 +162,102 @@
             for j in range(sub // col):
                 own[far[i], s, :, j * col:(j + 1) * col] = small_tile(chunk, s * sub + j * col)
 
-    for i in range(h):
+    pair = z // 2
+    pairs = Z // 2
+    mate = z + 1 - 2 * (z % 2)
+
+    def hand_on(i, yy, sending):
         k = near[i]
         zs = lo + k
 
-        @pl.when(zs != z)
-        def _():
-            for yy in range(2):
+        @pl.when((zs < z) & (z < Z - 1))
+        def _():
+            if sending:
                 arrived(act_e.at[k, yy], eC_r.at[k, yy])
-                @pl.when((zs < z) & (z < Z - 1))
-                def _():
-                    onward(k, yy, 1).start()
-
-                @pl.when((zs > z) & (z > 0))
-                def _():
-                    onward(k, yy, 0).start()
+                onward(k, yy, 1).start()
+            else:
+                onward(k, yy, 1).wait_send()
+
+        @pl.when((zs > z) & (z > 0))
+        def _():
+            if sending:
+                arrived(act_e.at[k, yy], eC_r.at[k, yy])
+                onward(k, yy, 0).start()
+            else:
+                onward(k, yy, 0).wait_send()
+
+    def last_stop(i, yy):
+        k = near[i]
+        zs = lo + k
+
+        @pl.when(((zs < z) & (z == Z - 1)) | ((zs > z) & (z == 0)))
+        def _():
+            arrived(act_e.at[k, yy], eC_r.at[k, yy])
+
+    def inside(i):
+        return (lo + far[i]) // 2 == pair
+
+    def nearer(i):
+        return jnp.where(lo + far[i] > z, z % 2 == 1, z % 2 == 0)
+
+    def home(i, cc):
+        return (lo + far[i] == z) & (c == cc)
 
     def z_copy(i, s, cc):
         k = far[i]
+        slot = jnp.where(inside(i) & (lo + k != z), pairs, pair)
         return rcopy(
-            zsend.at[k, s, cc], zrecv.at[z, s], z_s.at[k, s, cc], z_r.at[z, s], dev(cc, y, lo + k)
-        )
-
-    def home(i, cc):
-        return (lo + far[i] == z) & (c == cc)
-
+            zsend.at[k, s, cc], zrecv.at[slot, s], z_s.at[k, s, cc], z_r.at[slot, s], dev(cc, y, lo + k)
+        )
+
+    def p_copy(i, s):
+        k = far[i]
+        return rcopy(psend.at[k, s], precv.at[k, s], p_s.at[k, s], p_r.at[k, s], dev(c, y, mate))
+
+    def along_z(i, s):
+        k = far[i]
+        y_copy(i, s).wait_recv()
+        leaves = jnp.logical_not(inside(i)) & jnp.logical_not(nearer(i))
+
+        @pl.when(leaves)
+        def _():
+            psend[k, s] = (own[k, s] + yrecv[k, s].astype(F32)).astype(BF16)
+            p_copy(i, s).start()
+
+        @pl.when(inside(i))
+        def _():
+            for cc in range(2):
+                at = slice(cc * R, (cc + 1) * R)
+                zsend[k, s, cc] = (own[k, s, at, :] + yrecv[k, s, at, :].astype(F32)).astype(BF16)
+
+        @pl.when(jnp.logical_not(inside(i)) & nearer(i))
+        def _():
+            p_copy(i, s).wait_recv()
+            for cc in range(2):
+                at = slice(cc * R, (cc + 1) * R)
+                zsend[k, s, cc] = (
+                    own[k, s, at, :] + yrecv[k, s, at, :].astype(F32) + precv[k, s, at, :].astype(F32)
+                ).astype(BF16)
+
+        for cc in range(2):
+            @pl.when(home(i, cc))
+            def _():
+                pltpu.make_async_copy(zsend.at[k, s, cc], zrecv.at[pair, s], z_r.at[pair, s]).start()
+
+            @pl.when(jnp.logical_not(home(i, cc)) & jnp.logical_not(leaves))
+            def _():
+                z_copy(i, s, cc).start()
+
+    items = [(i, s) for i in range(h) for s in range(ns)]
+    for n in range(max(h, len(items))):
+        if n < h:
+            for yy in range(2):
+                hand_on(n, yy, True)
+        if n < len(items):
+            along_z(*items[n])
     for i in range(h):
-        k = far[i]
-        for s in range(ns):
-            y_copy(i, s).wait_recv()
-            for cc in range(2):
-                zsend[k, s, cc] = (
-                    own[k, s, cc * R:(cc + 1) * R, :] + yrecv[k, s, cc * R:(cc + 1) * R, :].astype(F32)
-                ).astype(BF16)
-
-                @pl.when(home(i, cc))
-                def _():
-                    pltpu.make_async_copy(zsend.at[k, s, cc], zrecv.at[z, s], z_r.at[z, s]).start()
-
-                @pl.when(jnp.logical_not(home(i, cc)))
-                def _():
-                    z_copy(i, s, cc).start()
+        for yy in range(2):
+            last_stop(i, yy)
 
     we_copy.wait()
     ecol = min(512, Vt)
@@ -224,14 +279,14 @@
     ep_copy = rcopy(epart.at[oc], erecv, ep_s, ep_r, dev(oc, y, z))
     ep_copy.start()
 
-    for zz in range(Z):
+    for zz in range(pairs + 1):
         for s in range(ns):
             arrived(zrecv.at[zz, s], z_r.at[zz, s])
     ep_copy.wait_recv()
     for s in range(ns):
         at = slice(s * sub, (s + 1) * sub)
         acc = zrecv[0, s].astype(F32)
-        for zz in range(1, Z):
+        for zz in range(1, pairs + 1):
             acc = acc + zrecv[zz, s].astype(F32)
         out_ref[:, at] = acc + (epart[c, :, at] + erecv[:, at])
 
@@ -246,22 +301,27 @@
     def _():
         to_core.wait_send()
 
+    @pl.when(cz == c)
+    def _():
+        for yy in range(2):
+            for up in range(2):
+                @pl.when((z < Z - 1) if up else (z > 0))
+                def _():
+                    onward(zk, yy, up).wait_send()
+
     for i in range(h):
-        k = near[i]
-        zs = lo + k
         for yy in range(2):
-            @pl.when((zs <= z) & (z < Z - 1))
-            def _():
-                onward(k, yy, 1).wait_send()
-
-            @pl.when((zs >= z) & (z > 0))
-            def _():
-                onward(k, yy, 0).wait_send()
-    for i in range(h):
+            hand_on(i, yy, False)
+        leaves = jnp.logical_not(inside(i)) & jnp.logical_not(nearer(i))
         for s in range(ns):
             y_copy(i, s).wait_send()
+
+            @pl.when(leaves)
+            def _():
+                p_copy(i, s).wait_send()
+
             for cc in range(2):
-                @pl.when(jnp.logical_not(home(i, cc)))
+                @pl.when(jnp.logical_not(home(i, cc)) & jnp.logical_not(leaves))
                 def _():
                     z_copy(i, s, cc).wait_send()
     ep_copy.wait_send()
@@ -296,7 +356,9 @@
             pltpu.VMEM((h, ns, 2 * R, sub), BF16),
             pltpu.VMEM((h, ns, 2 * R, sub), F32),
             pltpu.VMEM((h, ns, 2, R, sub), BF16),
-            pltpu.VMEM((T // 2, ns, R, sub), BF16),
+            pltpu.VMEM((T // 4 + 1, ns, R, sub), BF16),
+            pltpu.VMEM((h, ns, 2 * R, sub), BF16),
+            pltpu.VMEM((h, ns, 2 * R, sub), BF16),
             pltpu.VMEM((2, R, Vt), F32),
             pltpu.VMEM((R, Vt), F32),
             dma, dma((T // 2,)),
@@ -305,7 +367,8 @@
             dma((2,)), dma((2, 2)),
             dma((h, 2, 2)), dma((h, 2)),
             dma((h, ns)), dma((h, ns)),
-            dma((h, ns, 2)), dma((T // 2, ns)),
+            dma((h, ns, 2)), dma((T // 4 + 1, ns)),
+            dma((h, ns)), dma((h, ns)),
             dma, dma,
         ],
         compiler_params=pltpu.CompilerParams(
@@ -313,7 +376,7 @@
         ),
         cost_estimate=pl.CostEstimate(flops=flops, bytes_accessed=2 * 2 * Dh * Vt, transcendentals=0),
     )(
-        xe, gain.reshape(T, 1, De), xs, sgain.reshape(2, 1, Ds), we, ws.reshape(2 * Ds, ws.shape[2])
+        xe, gain.reshape(T, 1, De), xs, sgain, we, ws.reshape(2 * Ds, ws.shape[2])
     )
 
 

time: 104 us -> 86.5 us (0.83)
  the two profiles are of different devices: /device:TPU:21 before, /device:TPU:4 now
where the time goes in v2:
time: 86.5 us; the launch traced here: 86.3 us
  Pallas kernels  84 us (97%)
  local copies, waits for them, and re-layouts  2.3 us (3%)
    pallas_call x1, Pallas kernels, on_device(): pl.pallas_call(functools.partial(kernel, T, D, DS, ns), out_shape=jax.Sha...  84 us
    unnamed x1, local copies, waits for them, and re-layouts  2.3 us

profile of v2, /device:TPU:4, one launch (start us, length us, event | category | flops | bytes accessed | tf_op | source)
XLA Modules:
  0.0 86.3 jit_solution(10518499699048442183)
XLA Ops:
  0.0 84.0 %shard_map.64 = f32[128,2048]{1,0:T(8,128)} custom-call(bf16[128,1024]{1,0:T(8,128)(2,1)} %xe_ref.1, f32[8,1,1024]{2,1,0:T(1,128)} %bitcast.3, bf16[2,128,512]{2,1,0:T(8,128)(2,1)} %xs_ref.1, f32[2,512]{1,0:T(2,128)} %sgain_ref.1, bf16[4096,2048]{1,0:T(8,128)(2,1)} %we_hbm.1, bf16[1024,8192]{1,0:T(8,128)(2,1)} %bitcast.2), custom_call_target="tpu_custom_call" | custom-call | flops 8589934592 | bytes 33554432 | tf_op jit(solution)/shard_map/pallas_call | solution.py:342
  84.0 2.3 %copy.8 = f32[128,2048]{1,0:T(8,128)} copy(f32[128,2048]{1,0:T(8,128)} %shard_map.64) | data formatting | bytes 2097152

commit v3 on v2

--- a/solution.py
+++ b/solution.py
@@ -15,12 +15,12 @@
 def kernel(
     T, D, DS, ns,
     xe_ref, gain_ref, xs_ref, sgain_ref, we_hbm, ws_hbm, out_ref,
-    we_v, ws_v, xe_n, act_e, act_s, stat_out, stat_in, ysend, yrecv, own, zsend, zrecv, psend, precv, epart, erecv,
-    we_sem, ws_sem, st_s, st_r, as_s, as_r, eA_s, eA_r, eC_s, eC_r, y_s, y_r, z_s, z_r, p_s, p_r, ep_s, ep_r,
+    we_v, ws_v, act_n, scales, act_e, act_s, stat_out, stat_in, ysend, yrecv, own, zsend, zrecv, psend, precv, epart, erecv,
+    we_sem, ws_sem, st_s, st_r, as_s, as_r, sc_s, sc_r, eA_s, eA_r, eC_s, eC_r, y_s, y_r, z_s, z_r, p_s, p_r, ep_s, ep_r,
 ):
     Z = T // 2
     h = Z // 2
-    R, De = xe_n.shape
+    R, De = xe_ref.shape
     Ds = xs_ref.shape[2]
     Vt = out_ref.shape[1]
     sub = Vt // ns
@@ -94,6 +94,37 @@
     def _(i):
         stat_copy(i).start()
 
+    to_core = rcopy(xe_ref, act_e.at[zk, y, c], eA_s.at[0], eA_r.at[y, c], dev(cz, y, z))
+    across = rcopy(xe_ref, act_e.at[zk, y, c], eA_s.at[1], eA_r.at[y, c], dev(cz, oy, z))
+
+    @pl.when(cz == c)
+    def _():
+        pltpu.make_async_copy(xe_ref, act_e.at[zk, y, c], eA_r.at[y, c]).start()
+
+    @pl.when(cz != c)
+    def _():
+        to_core.start()
+
+    across.start()
+
+    def onward(k, yy, up):
+        return rcopy(
+            act_e.at[k, yy], act_e.at[k, yy], eC_s.at[k, yy, up], eC_r.at[k, yy],
+            dev(c, y, z + 1 if up else z - 1),
+        )
+
+    def set_out(yy):
+        @pl.when(cz == c)
+        def _():
+            for cc in range(2):
+                arrived(act_e.at[zk, yy, cc], eA_r.at[yy, cc])
+            for up in range(2):
+                @pl.when((z < Z - 1) if up else (z > 0))
+                def _():
+                    onward(zk, yy, up).start()
+
+    set_out(y)
+
     total = stat_out[...]
     for i in range(1, T):
         o = lax.rem(t + i, T)
@@ -107,35 +138,9 @@
     act_s[c, :, Ds:2 * Ds] = -((x1 * scale[:, 2:3] * sgain_ref[1:2, :]).astype(BF16))
     as_copy = rcopy(act_s.at[c], act_s.at[c], as_s, as_r, dev(oc, y, z))
     as_copy.start()
-
-    xe_n[...] = (xe * scale[:, 0:1] * gain_ref[t]).astype(BF16)
-    across = rcopy(xe_n, act_e.at[zk, y, c], eA_s.at[1], eA_r.at[y, c], dev(cz, oy, z))
-    across.start()
-    to_core = rcopy(xe_n, act_e.at[zk, y, c], eA_s.at[0], eA_r.at[y, c], dev(cz, y, z))
-
-    @pl.when(cz == c)
-    def _():
-        pltpu.make_async_copy(xe_n, act_e.at[zk, y, c], eA_r.at[y, c]).start()
-
-    @pl.when(cz != c)
-    def _():
-        to_core.start()
-
-    def onward(k, yy, up):
-        return rcopy(
-            act_e.at[k, yy], act_e.at[k, yy], eC_s.at[k, yy, up], eC_r.at[k, yy],
-            dev(c, y, z + 1 if up else z - 1),
-        )
-
-    @pl.when(cz == c)
-    def _():
-        for yy in range(2):
-            for cc in range(2):
-                arrived(act_e.at[zk, yy, cc], eA_r.at[yy, cc])
-            for up in range(2):
-                @pl.when((z < Z - 1) if up else (z > 0))
-                def _():
-                    onward(zk, yy, up).start()
+    scales[c] = scale
+    sc_copy = rcopy(scales.at[c], scales.at[c], sc_s, sc_r, dev(oc, y, z))
+    sc_copy.start()
 
     as_copy.wait_recv()
 
@@ -154,6 +159,8 @@
             for j in range(sub // col):
                 ysend[far[i], s, :, j * col:(j + 1) * col] = small_tile(chunk, s * sub + j * col).astype(BF16)
             y_copy(i, s).start()
+        if i == 0:
+            set_out(oy)
 
     for i in range(h):
         chunk = far[i] * 2 + y
@@ -248,33 +255,41 @@
             def _():
                 z_copy(i, s, cc).start()
 
-    items = [(i, s) for i in range(h) for s in range(ns)]
-    for n in range(max(h, len(items))):
-        if n < h:
-            for yy in range(2):
-                hand_on(n, yy, True)
-        if n < len(items):
-            along_z(*items[n])
-    for i in range(h):
+    ecol = min(512, Vt)
+
+    def expert(i):
+        k = near[i]
         for yy in range(2):
             last_stop(i, yy)
-
-    we_copy.wait()
-    ecol = min(512, Vt)
-
-    @pl.loop(0, Vt // ecol)
-    def _(j):
-        at = pl.ds(pl.multiple_of(j * ecol, ecol), ecol)
-        acc = jnp.zeros((2 * R, ecol), F32)
-        for k in range(h):
+            for cc in range(2):
+                rows = act_e[k, yy, cc].astype(F32)
+                act_n[yy, cc * R:(cc + 1) * R, :] = (
+                    rows * scales[cc, :, 0:1] * gain_ref[(lo + k) * 2 + yy]
+                ).astype(BF16)
+
+        @pl.loop(0, Vt // ecol)
+        def _(j):
+            at = pl.ds(pl.multiple_of(j * ecol, ecol), ecol)
+            acc = jnp.zeros((2 * R, ecol), F32)
             for yy in range(2):
-                b = k * 2 + yy
-                acc = acc + jnp.dot(
-                    act_e[k, yy].reshape(2 * R, De), we_v[b * De:(b + 1) * De, at],
-                    preferred_element_type=F32,
-                )
-        epart[0, :, at] = acc[0:R]
-        epart[1, :, at] = acc[R:2 * R]
+                depth = pl.ds(pl.multiple_of((k * 2 + yy) * De, De), De)
+                acc = acc + jnp.dot(act_n[yy], we_v[depth, at], preferred_element_type=F32)
+            for cc in range(2):
+                part = acc[cc * R:(cc + 1) * R]
+                epart[cc, :, at] = part if i == 0 else epart[cc, :, at] + part
+
+    items = [(i, s) for i in range(h) for s in range(ns)]
+    for n in range(len(items)):
+        if n < h:
+            for yy in (y, oy):
+                hand_on(n, yy, True)
+        if n == len(items) - 2:
+            sc_copy.wait_recv()
+            we_copy.wait()
+            for i in range(h - 1):
+                expert(i)
+        along_z(*items[n])
+    expert(h - 1)
 
     ep_copy = rcopy(epart.at[oc], erecv, ep_s, ep_r, dev(oc, y, z))
     ep_copy.start()
@@ -295,6 +310,7 @@
         stat_copy(i).wait_send()
 
     as_copy.wait_send()
+    sc_copy.wait_send()
     across.wait_send()
 
     @pl.when(cz != c)
@@ -333,7 +349,7 @@
     Dh, Vt = we.shape
     D, DS = De * T, Ds * T
     h = T // 4
-    ns = 2 if Vt >= 1024 else 1
+    ns = 4 if Vt >= 1024 else 1
     sub = Vt // ns
     vmem = pl.BlockSpec(memory_space=pltpu.VMEM)
     hbm = pl.BlockSpec(memory_space=pl.ANY)
@@ -347,7 +363,8 @@
         scratch_shapes=[
             pltpu.VMEM((Dh, Vt), BF16),
             pltpu.VMEM((T // 2, 2 * Ds, Vt), BF16),
-            pltpu.VMEM((R, De), BF16),
+            pltpu.VMEM((2, 2 * R, De), BF16),
+            pltpu.VMEM((2, R, R), F32),
             pltpu.VMEM((h, 2, 2, R, De), BF16),
             pltpu.VMEM((2, R, 2 * Ds), BF16),
             pltpu.VMEM((8, R), F32),
@@ -364,6 +381,7 @@
             dma, dma((T // 2,)),
             dma((T,)), dma((T,)),
             dma, dma,
+            dma, dma,
             dma((2,)), dma((2, 2)),
             dma((h, 2, 2)), dma((h, 2)),
             dma((h, ns)), dma((h, ns)),

time: 86.5 us -> 77.1 us (0.89); the launches traced: 86.3 us -> 76 us
  Pallas kernels: 84 us -> 73.7 us
    pallas_call x1, Pallas kernels: 84 us -> 73.7 us  [on_device(): pl.pallas_call(functools.partial(kernel, T, D, DS, ns), out_shape=jax.Sha...]
where the time goes in v3:
time: 77.1 us; the launch traced here: 76 us
  Pallas kernels  73.7 us (96%)
  local copies, waits for them, and re-layouts  2.3 us (3%)
    pallas_call x1, Pallas kernels, on_device(): pl.pallas_call(functools.partial(kernel, T, D, DS, ns), out_shape=jax.Sha...  73.7 us
    unnamed x1, local copies, waits for them, and re-layouts  2.3 us

profile of v3, /device:TPU:4, one launch (start us, length us, event | category | flops | bytes accessed | tf_op | source)
XLA Modules:
  0.0 76.0 jit_solution(10637579382236802076)
XLA Ops:
  0.0 73.7 %shard_map.64 = f32[128,2048]{1,0:T(8,128)} custom-call(bf16[128,1024]{1,0:T(8,128)(2,1)} %xe_ref.1, f32[8,1,1024]{2,1,0:T(1,128)} %bitcast.3, bf16[2,128,512]{2,1,0:T(8,128)(2,1)} %xs_ref.1, f32[2,512]{1,0:T(2,128)} %sgain_ref.1, bf16[4096,2048]{1,0:T(8,128)(2,1)} %we_hbm.1, bf16[1024,8192]{1,0:T(8,128)(2,1)} %bitcast.2), custom_call_target="tpu_custom_call" | custom-call | flops 8589934592 | bytes 33554432 | tf_op jit(solution)/shard_map/pallas_call | solution.py:358
  73.7 2.3 %copy.8 = f32[128,2048]{1,0:T(8,128)} copy(f32[128,2048]{1,0:T(8,128)} %shard_map.64) | data formatting | bytes 2097152
